TPU v7x, 128 devices: a whole 4x4x4 slice. The times are simulated.
128 devices in a mesh: row: 16 (over y, x_lo, core), col: 8 (over x_hi, z).
Axes of the slice: x: 4 (x_hi: 2, x_lo: 2; x = x_hi * 2 + x_lo), y: 4, z: 4, core: 2. Of those that a mesh axis runs over, the one named last changes fastest.
Arguments:
- tokens: bfloat16 [256, 2048, 256], P('row', 'col'), may hold values from -6 to 6
- bn_scale: float32 [256], replicated, may hold values from 0.5 to 1.5
- bn_shift: float32 [256], replicated, may hold values from -3 to 3
- w_expand: bfloat16 [256, 1024], replicated, may hold values from -0.375 to 0.375
- b_expand: float32 [1024], replicated, may hold values from -3 to 3
- dw_kernel: float32 [3, 3, 1024], replicated, may hold values from -2 to 2
- dw_bias: float32 [1024], replicated, may hold values from -3 to 3
- w_project: bfloat16 [1024, 256], replicated, may hold values from -0.1875 to 0.1875
- b_project: float32 [256], replicated, may hold values from -3 to 3
- norm_gains: float32 [4, 256], replicated, may hold values from 0.5 to 1.5
- attn_qkv: bfloat16 [2, 256, 768], replicated, may hold values from -0.375 to 0.375
- attn_out: bfloat16 [2, 256, 256], replicated, may hold values from -0.375 to 0.375
- rel_bias: float32 [2, 8, 225], replicated, may hold values from -5 to 762
- mlp_up: bfloat16 [2, 256, 1024], replicated, may hold values from -0.375 to 0.375
- mlp_down: bfloat16 [2, 1024, 256], replicated, may hold values from -0.1875 to 0.1875
Outputs:
- block_out: bfloat16 [256, 2048, 256], P('row', 'col')
All inputs are finite; a program needn't handle non-finite values.
Results may differ from a plain program's by a relative error of at most 0.018.
Values may be sent and summed in bfloat16 or wider, within the bound.
A program may use at most 128 MiB of HBM per device.

v0:
```python
import jax
import jax.numpy as jnp
from jax import lax
from jax.sharding import PartitionSpec as P

WIN = 8
GRID = 8


def extended(block, sides, width):
    for axis, dim in sides:
        count = lax.axis_size(axis)
        forward = [(i, i + 1) for i in range(count - 1)]
        backward = [(target, source) for source, target in forward]
        low = lax.ppermute(
            lax.slice_in_dim(block, block.shape[dim] - width, None, axis=dim), axis, forward
        )
        high = lax.ppermute(lax.slice_in_dim(block, 0, width, axis=dim), axis, backward)
        block = jnp.concatenate([low, block, high], axis=dim)
    return block


def table_index(window):
    places = jnp.arange(window * window, dtype=jnp.int32)
    across = places // window
    within = places % window
    row_part = (across[:, None] - across[None, :] + window - 1) * (2 * window - 1)
    return row_part + (within[:, None] - within[None, :] + window - 1)


def bias_table(rel_section, window):
    position_index = table_index(window).reshape(1, -1)
    n_entries = rel_section.shape[1]
    onehot = (jnp.arange(n_entries, dtype=jnp.int32)[:, None] == position_index).astype(jnp.float32)
    lookup = jnp.dot(rel_section, onehot, precision=lax.Precision.HIGHEST)
    return lookup.reshape(rel_section.shape[0], window * window, window * window)


def layer_norm(values, gain):
    center = values - jnp.mean(values, axis=-1, keepdims=True)
    spread = jnp.mean(center * center, axis=-1, keepdims=True)
    return center * lax.rsqrt(spread + 1e-05) * gain


def attend(windows, gain, w_qkv, w_out, bias_full):
    n_windows, per_window, features = windows.shape
    n_heads = bias_full.shape[0]
    head_size = features // n_heads
    values = windows.astype(jnp.float32)
    normed = layer_norm(values, gain).astype(jnp.bfloat16)
    packed = jnp.dot(
        normed.reshape(-1, features), w_qkv, preferred_element_type=jnp.float32
    ).astype(jnp.bfloat16)
    packed = packed.reshape(n_windows, per_window, 3, n_heads, head_size)
    queries = packed[:, :, 0]
    key_part = packed[:, :, 1]
    value_part = packed[:, :, 2]
    scores = jnp.einsum("nqhd,nkhd->nhqk", queries, key_part, preferred_element_type=jnp.float32)
    scores = scores * head_size ** (-0.5) + bias_full[None]
    weights = jax.nn.softmax(scores, axis=-1).astype(jnp.bfloat16)
    context = jnp.einsum(
        "nhqk,nkhd->nqhd", weights, value_part, preferred_element_type=jnp.float32
    ).astype(jnp.bfloat16)
    context = context.reshape(-1, features)
    result = values.reshape(-1, features) + jnp.dot(
        context, w_out, preferred_element_type=jnp.float32
    )
    return result.astype(jnp.bfloat16).reshape(n_windows, per_window, features)


def feed_forward(flat, gain, w_up, w_down):
    values = flat.astype(jnp.float32)
    normed = layer_norm(values, gain).astype(jnp.bfloat16)
    inner_act = jax.nn.gelu(jnp.dot(normed, w_up, preferred_element_type=jnp.float32)).astype(
        jnp.bfloat16
    )
    return (values + jnp.dot(inner_act, w_down, preferred_element_type=jnp.float32)).astype(
        jnp.bfloat16
    )


def expand_tokens(source, bn_scale, bn_shift, w_expand, b_expand):
    tall, broad, features = source.shape
    normed = (source.astype(jnp.float32) * bn_scale + bn_shift).astype(jnp.bfloat16)
    inner_act = (
        jnp.dot(normed.reshape(-1, features), w_expand, preferred_element_type=jnp.float32)
        + b_expand
    )
    return jax.nn.gelu(inner_act).astype(jnp.bfloat16).reshape(tall, broad, -1)


def to_windows(received, shape_info):
    row_devs, col_devs, row_classes, col_classes, row_stack, col_stack = shape_info
    features = received.shape[-1]
    part_windows = received.shape[1]
    arranged = received.reshape(
        row_devs // row_classes,
        row_classes,
        col_devs // col_classes,
        col_classes,
        part_windows,
        row_stack,
        col_stack,
        features,
    )
    arranged = arranged.transpose(1, 3, 4, 0, 5, 2, 6, 7)
    return arranged.reshape(row_classes * col_classes * part_windows, -1, features)


def from_windows(finished, part_windows, shape_info):
    row_devs, col_devs, row_classes, col_classes, row_stack, col_stack = shape_info
    features = finished.shape[-1]
    arranged = finished.reshape(
        row_classes,
        col_classes,
        part_windows,
        row_devs // row_classes,
        row_stack,
        col_devs // col_classes,
        col_stack,
        features,
    )
    arranged = arranged.transpose(3, 0, 5, 1, 2, 4, 6, 7)
    return arranged.reshape(row_devs * col_devs, part_windows, row_stack * col_stack, features)


def on_device(
    tokens,
    bn_scale,
    bn_shift,
    w_expand,
    b_expand,
    dw_kernel,
    dw_bias,
    w_project,
    b_project,
    norm_gains,
    attn_qkv,
    attn_out,
    rel_bias,
    mlp_up,
    mlp_down,
):
    tile_r, tile_c, features = tokens.shape
    n_row = lax.axis_size("row")
    n_col = lax.axis_size("col")
    hidden = expand_tokens(tokens, bn_scale, bn_shift, w_expand, b_expand)
    padded = extended(hidden, (("row", 0), ("col", 1)), 1)
    summed = jnp.zeros((tile_r, tile_c, padded.shape[2]), jnp.float32) + dw_bias
    for off_r in range(3):
        for off_c in range(3):
            summed = (
                summed
                + padded[off_r : off_r + tile_r, off_c : off_c + tile_c].astype(jnp.float32)
                * dw_kernel[off_r, off_c]
            )
    activated = jax.nn.gelu(summed).astype(jnp.bfloat16).reshape(tile_r * tile_c, -1)
    conv_sum = (
        tokens.reshape(-1, features).astype(jnp.float32)
        + jnp.dot(activated, w_project, preferred_element_type=jnp.float32)
        + b_project
    )
    after_conv = conv_sum.astype(jnp.bfloat16).reshape(tile_r, tile_c, features)
    blocks = after_conv.reshape(tile_r // WIN, WIN, tile_c // WIN, WIN, features).transpose(
        0, 2, 1, 3, 4
    )
    blocks = blocks.reshape(-1, WIN * WIN, features)
    after_block = attend(
        blocks, norm_gains[0], attn_qkv[0], attn_out[0], bias_table(rel_bias[0], WIN)
    )
    after_block = after_block.reshape(tile_r // WIN, tile_c // WIN, WIN, WIN, features).transpose(
        0, 2, 1, 3, 4
    )
    after_mlp = feed_forward(
        after_block.reshape(-1, features), norm_gains[1], mlp_up[0], mlp_down[0]
    )
    stride_r = tile_r * n_row // GRID
    stride_c = tile_c * n_col // GRID
    high_r = min(tile_r, stride_r)
    high_c = min(tile_c, stride_c)
    row_stack = tile_r // high_r
    col_stack = tile_c // high_c
    shape_info = (n_row, n_col, stride_r // high_r, stride_c // high_c, row_stack, col_stack)
    devices = n_row * n_col
    part_windows = high_r * high_c // devices
    local_parts = after_mlp.reshape(row_stack, high_r, col_stack, high_c, features).transpose(
        1, 3, 0, 2, 4
    )
    local_parts = local_parts.reshape(devices, part_windows, row_stack * col_stack, features)
    grid_bias = bias_table(rel_bias[1], GRID)
    sectioned_in = lax.all_to_all(
        lax.all_to_all(
            local_parts.reshape(n_row, n_col, part_windows, -1, features),
            "row",
            split_axis=0,
            concat_axis=0,
            tiled=True,
        ),
        "col",
        split_axis=1,
        concat_axis=1,
        tiled=True,
    )
    received = sectioned_in.reshape(devices, part_windows, -1, features)
    windows = to_windows(received, shape_info)
    finished = attend(windows, norm_gains[2], attn_qkv[1], attn_out[1], grid_bias)
    attended = from_windows(finished, received.shape[1], shape_info)
    returned = lax.all_to_all(
        lax.all_to_all(
            attended.reshape(n_row, n_col, part_windows, -1, features),
            "row",
            split_axis=0,
            concat_axis=0,
            tiled=True,
        ),
        "col",
        split_axis=1,
        concat_axis=1,
        tiled=True,
    )
    after_grid = returned.reshape(high_r, high_c, row_stack, col_stack, features).transpose(
        2, 0, 3, 1, 4
    )
    block_out = feed_forward(
        after_grid.reshape(-1, features), norm_gains[3], mlp_up[1], mlp_down[1]
    )
    return block_out.reshape(tile_r, tile_c, features)


def solution(mesh):
    placed = (
        P("row", "col", None),
        P(),
        P(),
        P(),
        P(),
        P(),
        P(),
        P(),
        P(),
        P(),
        P(),
        P(),
        P(),
        P(),
        P(),
    )
    return jax.shard_map(
        on_device, mesh=mesh, in_specs=placed, out_specs=P("row", "col", None), check_vma=False
    )
```

profile of v0, /device:TPU:0, one launch (start us, length us, event | category | flops | bytes accessed | tf_op | source)
XLA Modules:
  0.0 497.4 jit_solution(17017590422353367850)
XLA Ops:
  2.3 8.8 %fusion.9 = bf16[4096,1024]{1,0:T(8,128)(2,1)} fusion(bf16[4096,256]{1,0:T(8,128)(2,1)S(1)} %bitcast.175, bf16[256,1024]{1,0:T(8,128)(2,1)S(1)} %copy-done, f32[1024]{0:T(1024)} %param.19), kind=kOutput, calls=%fused_computation.13 | convolution fusion | flops 2189426688 | bytes 11014144 | tf_op jit(solution)/shard_map/dot_general | solution.py:86
  20.6 3.8 collective-permute-start.2
  27.3 3.4 collective-permute-done.3
  30.7 17.1 %maximum_maximum_fusion = (bf16[18,257,1024]{2,1,0:T(8,128)(2,1)S(1)}, bf16[18,257,1024]{2,1,0:T(8,128)(2,1)}) fusion(bf16[1,256,1024]{2,1,0:T(8,128)(2,1)} %copy-done.4, bf16[16,256,1024]{2,1,0:T(8,128)(2,1)} %bitcast.3, bf16[1,256,1024]{2,1,0:T(8,128)(2,1)} %copy-done.3, bf16[18,1,1024]{2,1,0:T(2,128)(2,1)S(1)} %collective-permute-done.2, ...), kind=kLoop, calls=%fused_computation.46 | loop fusion | flops 75792384 | bytes 28459008 | tf_op jit(solution)/shard_map/concatenate | solution.py:19
  47.8 30.6 %fusion.17 = bf16[16,256,1024]{2,1,0:T(8,128)(2,1)} fusion(bf16[16,256,1024]{2,1,0:T(8,128)(2,1)} %bitcast.3, bf16[18,257,1024]{2,1,0:T(8,128)(2,1)} %get-tuple-element.12, bf16[1,256,1024]{2,1,0:T(8,128)(2,1)} %copy-done.4, bf16[18,257,1024]{2,1,0:T(8,128)(2,1)S(1)} %get-tuple-element.11, bf16[1,256,1024]{2,1,0:T(8,128)(2,1)} %copy-done.3, ...), kind=kLoop, calls=%fused_computation.21 | loop fusion | flops 159383552 | bytes 68198400 | tf_op jit(solution)/shard_map/convert_element_type | solution.py:157
  78.4 6.5 %fusion.63 = bf16[4096,256]{1,0:T(8,128)(2,1)S(1)} fusion(bf16[4096,1024]{1,0:T(8,128)(2,1)} %bitcast.168, bf16[1024,256]{1,0:T(8,128)(2,1)} %param.22, f32[256]{0:T(256)S(1)} %copy-done.19, bf16[4096,256]{1,0:T(8,128)(2,1)} %bitcast.174), kind=kOutput, calls=%fused_computation.70 | convolution fusion | flops 2151677952 | bytes 13108224 | tf_op jit(solution)/shard_map/dot_general | solution.py:160
  88.9 4.5 convolution_convert_fusion.1
  93.3 8.6 %copy.73 = bf16[4096,768]{0,1:T(8,128)(2,1)} copy(bf16[4096,768]{1,0:T(8,128)(2,1)} %convolution_convert_fusion.1) | data formatting | bytes 12582912 | tf_op jit(solution)/shard_map/convert_element_type | solution.py:53
  101.9 18.4 %reshape.337 = bf16[64,64,3,8,32]{1,0,4,3,2:T(8,128)(2,1)} reshape(bf16[4096,768]{0,1:T(8,128)(2,1)} %copy.73) | data formatting | bytes 12582912 | tf_op jit(solution)/shard_map/reshape | solution.py:54
  120.3 8.3 %fusion.105 = (bf16[64,64,1,8,32]{1,0,4,3,2:T(8,128)(2,1)}, bf16[64,64,1,8,32]{1,0,4,3,2:T(8,128)(2,1)S(1)}, bf16[64,64,1,8,32]{1,0,4,3,2:T(8,128)(2,1)}) fusion(bf16[64,64,3,8,32]{1,0,4,3,2:T(8,128)(2,1)} %reshape.337), kind=kLoop, calls=%fused_computation.155 | loop fusion | bytes 12582912 | tf_op jit(solution)/shard_map/slice | solution.py:57
  128.6 19.1 %fusion.67 = f32[64,8,64,64]{2,3,1,0:T(8,128)} fusion(bf16[64,64,1,8,32]{1,0,4,3,2:T(8,128)(2,1)} %get-tuple-element.10, bf16[64,64,1,8,32]{1,0,4,3,2:T(8,128)(2,1)S(1)} %get-tuple-element.9), kind=kOutput, calls=%fused_computation.80 | convolution fusion | flops 134217728 | bytes 12582912 | tf_op jit(solution)/shard_map/nqhd,nkhd->nhqk/dot_general | solution.py:58
  147.8 17.8 %fusion.108 = (f32[64,8,64]{2,1,0:T(8,128)S(1)}, f32[64,8,64,64]{2,3,1,0:T(8,128)}) fusion(f32[64,8,64,64]{2,3,1,0:T(8,128)} %fusion.67, f32[8,64,64]{1,2,0:T(8,128)S(1)} %copy-done.5), kind=kOutput, calls=%fused_computation.158 | output fusion | flops 12582975 | bytes 17039360 | tf_op jit(solution)/shard_map/sub | solution.py:60
  165.5 18.0 %convert_bitcast_fusion.1 = bf16[64,64,8,32]{1,3,2,0:T(8,128)(2,1)} fusion(f32[64,8,64,64]{2,3,1,0:T(8,128)} %get-tuple-element.31, f32[64,8,64]{2,1,0:T(8,128)S(1)} %get-tuple-element.30, bf16[64,64,1,8,32]{1,0,4,3,2:T(8,128)(2,1)} %get-tuple-element.8), kind=kOutput, calls=%fused_computation.96 | convolution fusion | flops 139460608 | bytes 12713984 | tf_op jit(solution)/shard_map/nhqk,nkhd->nqhd/dot_general | solution.py:61
  183.6 7.1 %copy.79 = bf16[64,64,8,32]{1,0,3,2:T(8,128)(2,1)} copy(bf16[64,64,8,32]{1,3,2,0:T(8,128)(2,1)} %convert_bitcast_fusion.1) | data formatting | bytes 4194304 | tf_op jit(solution)/shard_map/convert_element_type | solution.py:63
  190.6 6.7 %reshape.338 = bf16[4096,256]{0,1:T(8,128)(2,1)} reshape(bf16[64,64,8,32]{1,0,3,2:T(8,128)(2,1)} %copy.79) | data formatting | bytes 4194304 | tf_op jit(solution)/shard_map/reshape | solution.py:64
  206.1 9.0 %fusion.60 = bf16[4096,256]{1,0:T(8,128)(2,1)} fusion(f32[4096,256]{1,0:T(8,128)} %bitcast.170, bf16[4096,256]{1,0:T(8,128)(2,1)S(1)} %bitcast.171, bf16[2,1024,256]{2,1,0:T(8,128)(2,1)} %param.29, bf16[2,256,1024]{2,1,0:T(8,128)(2,1)} %param.28), kind=kOutput, calls=%fused_computation.69 | convolution fusion | flops 4334813184 | bytes 9437184 | tf_op jit(solution)/shard_map/dot_general | solution.py:77
  215.1 41.6 %all_to_all.20 = bf16[16,8,32,1,256]{4,2,1,3,0:T(8,128)(2,1)S(1)} all-to-all(bf16[16,8,32,1,256]{4,2,1,3,0:T(8,128)(2,1)} %bitcast.173), channel_id=1, replica_groups=mesh['row'=16,'col'=8] {'row'}, dimensions={0} | all-to-all | bytes 4194304 | tf_op jit(solution)/shard_map/all_to_all | solution.py:192
  258.2 8.8 %all-to-all-start.1 = ((bf16[16,8,32,1,256]{4,2,0,3,1:T(8,128)(2,1)}), bf16[16,8,32,1,256]{4,2,0,3,1:T(8,128)(2,1)S(1)}, u32[]{:S(2)}, u32[]{:S(2)}) async-start(bf16[16,8,32,1,256]{4,2,0,3,1:T(8,128)(2,1)} %copy.82), calls=%async_computation.1 | async-start | bytes 4194304 | tf_op jit(solution)/shard_map/all_to_all | solution.py:191
  268.6 24.3 %all-to-all-done.1 = bf16[16,8,32,1,256]{4,2,0,3,1:T(8,128)(2,1)S(1)} async-done(((bf16[16,8,32,1,256]{4,2,0,3,1:T(8,128)(2,1)}), bf16[16,8,32,1,256]{4,2,0,3,1:T(8,128)(2,1)S(1)}, u32[]{:S(2)}, u32[]{:S(2)}) %all-to-all-start.1) | async-done | bytes 2097184 | tf_op jit(solution)/shard_map/all_to_all | solution.py:191
  293.4 3.3 copy.83
  305.3 4.5 convolution_convert_fusion
  309.8 8.6 %copy.84 = bf16[4096,768]{0,1:T(8,128)(2,1)} copy(bf16[4096,768]{1,0:T(8,128)(2,1)} %convolution_convert_fusion) | data formatting | bytes 12582912 | tf_op jit(solution)/shard_map/convert_element_type | solution.py:53
  318.4 17.9 %reshape.339 = bf16[64,64,3,8,32]{1,0,4,3,2:T(8,128)(2,1)} reshape(bf16[4096,768]{0,1:T(8,128)(2,1)} %copy.84) | data formatting | bytes 12582912 | tf_op jit(solution)/shard_map/reshape | solution.py:54
  336.3 7.7 %fusion.104 = (bf16[64,64,1,8,32]{1,0,4,3,2:T(8,128)(2,1)}, bf16[64,64,1,8,32]{1,0,4,3,2:T(8,128)(2,1)S(1)}, bf16[64,64,1,8,32]{1,0,4,3,2:T(8,128)(2,1)S(1)}) fusion(bf16[64,64,3,8,32]{1,0,4,3,2:T(8,128)(2,1)} %reshape.339), kind=kLoop, calls=%fused_computation.154 | loop fusion | bytes 12582912 | tf_op jit(solution)/shard_map/slice | solution.py:57
  344.0 21.2 %fusion.66 = f32[64,8,64,64]{2,3,1,0:T(8,128)} fusion(bf16[64,64,1,8,32]{1,0,4,3,2:T(8,128)(2,1)S(1)} %get-tuple-element.7, bf16[64,64,1,8,32]{1,0,4,3,2:T(8,128)(2,1)S(1)} %get-tuple-element.6), kind=kOutput, calls=%fused_computation.76 | convolution fusion | flops 134217728 | bytes 12582912 | tf_op jit(solution)/shard_map/nqhd,nkhd->nhqk/dot_general | solution.py:58
  365.2 17.8 %fusion.109 = (f32[64,8,64]{2,1,0:T(8,128)S(1)}, f32[64,8,64,64]{2,3,1,0:T(8,128)}) fusion(f32[64,8,64,64]{2,3,1,0:T(8,128)} %fusion.66, f32[8,64,64]{1,2,0:T(8,128)S(1)} %copy.88), kind=kOutput, calls=%fused_computation.159 | output fusion | flops 12582975 | bytes 17039360 | tf_op jit(solution)/shard_map/sub | solution.py:60
  383.0 18.0 %convert_bitcast_fusion = bf16[64,64,8,32]{1,3,2,0:T(8,128)(2,1)} fusion(f32[64,8,64,64]{2,3,1,0:T(8,128)} %get-tuple-element.33, f32[64,8,64]{2,1,0:T(8,128)S(1)} %get-tuple-element.32, bf16[64,64,1,8,32]{1,0,4,3,2:T(8,128)(2,1)} %get-tuple-element.5), kind=kOutput, calls=%fused_computation.91 | convolution fusion | flops 139460608 | bytes 12713984 | tf_op jit(solution)/shard_map/nhqk,nkhd->nqhd/dot_general | solution.py:61
  401.0 7.1 %copy.90 = bf16[64,64,8,32]{1,0,3,2:T(8,128)(2,1)} copy(bf16[64,64,8,32]{1,3,2,0:T(8,128)(2,1)} %convert_bitcast_fusion) | data formatting | bytes 4194304 | tf_op jit(solution)/shard_map/convert_element_type | solution.py:63
  408.1 5.7 %reshape.340 = bf16[4096,256]{0,1:T(8,128)(2,1)S(1)} reshape(bf16[64,64,8,32]{1,0,3,2:T(8,128)(2,1)} %copy.90) | data formatting | bytes 4194304 | tf_op jit(solution)/shard_map/reshape | solution.py:64
  418.0 30.8 %all_to_all.21 = bf16[16,8,32,1,256]{4,2,1,3,0:T(8,128)(2,1)S(1)} all-to-all(bf16[16,8,32,1,256]{4,2,1,3,0:T(8,128)(2,1)S(1)} %bitcast.166), channel_id=1, replica_groups=mesh['row'=16,'col'=8] {'row'}, dimensions={0} | all-to-all | bytes 4194304 | tf_op jit(solution)/shard_map/all_to_all | solution.py:209
  449.1 33.0 %all_to_all.22 = bf16[16,8,32,1,256]{4,2,0,3,1:T(8,128)(2,1)S(1)} all-to-all(bf16[16,8,32,1,256]{4,2,0,3,1:T(8,128)(2,1)S(1)} %copy.93), channel_id=1, replica_groups=mesh['row'=16,'col'=8] {'col'}, dimensions={1} | all-to-all | bytes 4194304 | tf_op jit(solution)/shard_map/all_to_all | solution.py:208
  487.8 9.1 %fusion.57 = bf16[4096,256]{1,0:T(8,128)(2,1)} fusion(f32[4096,256]{1,0:T(8,128)} %bitcast.169, bf16[4096,256]{1,0:T(8,128)(2,1)S(1)} %bitcast.172, bf16[2,1024,256]{2,1,0:T(8,128)(2,1)} %param.29, bf16[2,256,1024]{2,1,0:T(8,128)(2,1)} %param.28), kind=kOutput, calls=%fused_computation.68 | convolution fusion | flops 4334813184 | bytes 9437184 | tf_op jit(solution)/shard_map/dot_general | solution.py:77
  (91 shorter events, 49.3 us)
Async XLA Ops:
  0.0 2.3 copy-start
  2.3 12.9 %copy-start.9 = (f32[3,3,1024]{2,1,0:T(4,128)S(1)}, f32[3,3,1024]{2,1,0:T(4,128)}, u32[]{:S(2)}) copy-start(f32[3,3,1024]{2,1,0:T(4,128)} %param.20) | copy-start | bytes 110596
  2.3 13.5 %copy-start.17 = (f32[2,8,225]{2,1,0:T(8,128)S(1)}, f32[2,8,225]{2,1,0:T(8,128)}, u32[]{:S(2)}) copy-start(f32[2,8,225]{2,1,0:T(8,128)} %param.27) | copy-start | bytes 43204
  11.1 14.7 %copy-start.16 = (f32[4,256]{1,0:T(4,128)S(1)}, f32[4,256]{1,0:T(4,128)}, u32[]{:S(2)}) copy-start(f32[4,256]{1,0:T(4,128)} %param.24) | copy-start | bytes 12292
  12.3 4.7 collective-permute-start
  13.7 5.6 %collective-permute-start.1 = (bf16[1,256,1024]{2,1,0:T(8,128)(2,1)S(1)}, bf16[1,256,1024]{2,1,0:T(8,128)(2,1)S(1)}, u32[]{:S(2)}, u32[]{:S(2)}) collective-permute-start(bf16[1,256,1024]{2,1,0:T(8,128)(2,1)S(1)} %get-tuple-element.16), channel_id=1, source_target_pairs={{8,0},{16,8},{24,16},{32,24},{40,32},{48,40},{56,48},{64,56},{72,6... | collective-permute-start | bytes 1572872 | tf_op jit(solution)/shard_map/ppermute | solution.py:18
  15.2 12.1 %copy-start.10 = (s32[4096]{0:T(1024)}, s32[4096]{0:T(1024)S(1)}, u32[]{:S(2)}) copy-start(s32[4096]{0:T(1024)S(1)} %add.239) | copy-start | bytes 49156
  17.1 10.2 %copy-start.3 = (bf16[1,256,1024]{2,1,0:T(8,128)(2,1)}, bf16[1,256,1024]{2,1,0:T(8,128)(2,1)S(1)}, u32[]{:S(2)}) copy-start(bf16[1,256,1024]{2,1,0:T(8,128)(2,1)S(1)} %collective-permute-done) | copy-start | bytes 1572868
  19.3 8.0 %copy-start.4 = (bf16[1,256,1024]{2,1,0:T(8,128)(2,1)}, bf16[1,256,1024]{2,1,0:T(8,128)(2,1)S(1)}, u32[]{:S(2)}) copy-start(bf16[1,256,1024]{2,1,0:T(8,128)(2,1)S(1)} %collective-permute-done.1) | copy-start | bytes 1572868
  20.6 6.7 %collective-permute-start.2 = (bf16[18,1,1024]{2,1,0:T(2,128)(2,1)S(1)}, bf16[18,1,1024]{2,1,0:T(2,128)(2,1)S(1)}, u32[]{:S(2)}, u32[]{:S(2)}) collective-permute-start(bf16[18,1,1024]{2,1,0:T(2,128)(2,1)S(1)} %get-tuple-element.13), channel_id=1, source_target_pairs={{0,1},{1,2},{2,3},{3,4},{4,5},{5,6},{6,7},{8,9},{9,10},{10,11},{11... | collective-permute-start | bytes 110600 | tf_op jit(solution)/shard_map/ppermute | solution.py:15
  24.4 6.2 %collective-permute-start.3 = (bf16[18,1,1024]{2,1,0:T(2,128)(2,1)S(1)}, bf16[18,1,1024]{2,1,0:T(2,128)(2,1)S(1)}, u32[]{:S(2)}, u32[]{:S(2)}) collective-permute-start(bf16[18,1,1024]{2,1,0:T(2,128)(2,1)S(1)} %get-tuple-element.14), channel_id=1, source_target_pairs={{1,0},{2,1},{3,2},{4,3},{5,4},{6,5},{7,6},{9,8},{10,9},{11,10},{12... | collective-permute-start | bytes 110600 | tf_op jit(solution)/shard_map/ppermute | solution.py:18
  47.8 30.6 %copy-start.19 = (f32[256]{0:T(256)S(1)}, f32[256]{0:T(256)}, u32[]{:S(2)}) copy-start(f32[256]{0:T(256)} %param.23) | copy-start | bytes 3076
  85.4 2.1 copy-start.15
  86.0 2.9 copy-start.6
  128.6 19.1 %copy-start.5 = (f32[8,64,64]{1,2,0:T(8,128)S(1)}, f32[8,64,64]{1,2,0:T(8,128)}, u32[]{:S(2)}) copy-start(f32[8,64,64]{1,2,0:T(8,128)} %copy.77) | copy-start | bytes 393220
  190.6 7.2 %copy-start.7 = (bf16[2,256,256]{2,1,0:T(8,128)(2,1)S(1)}, bf16[2,256,256]{2,1,0:T(8,128)(2,1)}, u32[]{:S(2)}) copy-start(bf16[2,256,256]{2,1,0:T(8,128)(2,1)} %param.26) | copy-start | bytes 786436
  197.3 1.6 copy-start.2
  200.8 3.8 copy-start.14
  215.1 52.0 %copy-start.11 = (s32[4096]{0:T(1024)S(1)}, s32[4096]{0:T(1024)}, u32[]{:S(2)}) copy-start(s32[4096]{0:T(1024)} %copy-done.10) | copy-start | bytes 49156
  215.1 52.0 %copy-start.18 = (f32[2,8,225]{2,1,0:T(8,128)S(1)}, f32[2,8,225]{2,1,0:T(8,128)}, u32[]{:S(2)}) copy-start(f32[2,8,225]{2,1,0:T(8,128)} %param.27) | copy-start | bytes 43204
  258.2 34.7 %all-to-all-start.1 = ((bf16[16,8,32,1,256]{4,2,0,3,1:T(8,128)(2,1)}), bf16[16,8,32,1,256]{4,2,0,3,1:T(8,128)(2,1)S(1)}, u32[]{:S(2)}, u32[]{:S(2)}) async-start(bf16[16,8,32,1,256]{4,2,0,3,1:T(8,128)(2,1)} %copy.82), calls=%async_computation.1 | async-start | bytes 4194304 | tf_op jit(solution)/shard_map/all_to_all | solution.py:191
  296.7 5.8 %copy-start.13 = (f32[1,256]{1,0:T(1,128)S(1)}, f32[1,256]{1,0:T(1,128)}, u32[]{:S(2)}) copy-start(f32[1,256]{1,0:T(1,128)} %get-tuple-element.29) | copy-start | bytes 3076
  401.0 12.8 %copy-start.8 = (bf16[2,256,256]{2,1,0:T(8,128)(2,1)S(1)}, bf16[2,256,256]{2,1,0:T(8,128)(2,1)}, u32[]{:S(2)}) copy-start(bf16[2,256,256]{2,1,0:T(8,128)(2,1)} %param.26) | copy-start | bytes 786436
  482.1 4.5 copy-start.12
  487.8 9.1 %copy-start.1 = (bf16[256,1024]{1,0:T(8,128)(2,1)S(1)}, bf16[256,1024]{1,0:T(8,128)(2,1)}, u32[]{:S(2)}) copy-start(bf16[256,1024]{1,0:T(8,128)(2,1)} %param.18) | copy-start | bytes 1572868
where the time goes:
time: 504 us; the launch traced here: 497 us
  matrix products  125 us (25%)
  local copies, waits for them, and re-layouts  110 us (22%)
  other arithmetic  109 us (22%)
  blocking collectives  106 us (21%)
  waiting for transfers between devices  29.9 us (6%)
  starting transfers between devices  16.6 us (3%)
    all_to_all x1, blocking collectives, on_device(): lax.all_to_all(local_parts.reshape(n_row, n_col, part_windows, -1, featur...  41.6 us
    dot_general x2, matrix products, attend(): jnp.einsum('nqhd,nkhd->nhqk', queries, key_part, preferred_element_type=j...  40.3 us
    reshape x2, local copies, waits for them, and re-layouts, attend(): packed = packed.reshape(n_windows, per_window, 3, n_heads, head_size)  36.3 us
    dot_general x2, matrix products, attend(): jnp.einsum('nhqk,nkhd->nqhd', weights, value_part, preferred_element_type...  36 us
    sub x2, other arithmetic, attend(): weights = jax.nn.softmax(scores, axis=-1).astype(jnp.bfloat16)  35.6 us
    all_to_all x1, blocking collectives, on_device(): lax.all_to_all(lax.all_to_all(attended.reshape(n_row, n_col, part_windows...  33 us
    all_to_all x1, blocking collectives, on_device(): lax.all_to_all(attended.reshape(n_row, n_col, part_windows, -1, features)...  30.8 us
    convert_element_type x1, other arithmetic, on_device(): jax.nn.gelu(summed).astype(jnp.bfloat16).reshape(tile_r * tile_c, -1)  30.6 us
  transfers between devices with their start and end apart: 5, of which 3 were waited for; matrix products, arithmetic and copies ran while one was open for 1% of the time, Pallas kernels for 0%

commit v1 on v0

v1 whole, which is shorter than its diff:
```python
import functools
import math

import jax
import jax.numpy as jnp
from jax import lax
from jax.experimental import pallas as pl
from jax.experimental.pallas import tpu as pltpu
from jax.sharding import PartitionSpec as P

WIN = 8
BF = jnp.bfloat16
F32 = jnp.float32
MESH = pl.DeviceIdType.MESH


def gelu(v):
    half = v * 0.5
    inner = v * (0.7978845608 + 0.0356774081 * (v * v))
    return half + half * jnp.tanh(inner)


def dot(a, b):
    return jnp.dot(a, b, preferred_element_type=F32)


def layer_norm(x, gain):
    center = x - jnp.mean(x, axis=-1, keepdims=True)
    spread = jnp.mean(center * center, axis=-1, keepdims=True)
    return (center * lax.rsqrt(spread + 1e-05) * gain).astype(BF)


def attend_and_mlp(x, gain_a, gain_m, w_qkv, w_out, bias, w_up, w_down, head_masks, n_windows):
    qkv = dot(layer_norm(x, gain_a), w_qkv[...])
    q = (qkv[:, :256] * (math.log2(math.e) / math.sqrt(32.0))).astype(BF)
    k = qkv[:, 256:512].astype(BF)
    v = qkv[:, 512:].astype(BF)
    low = lax.broadcasted_iota(jnp.int32, (64, 128), 1) < 64
    contexts = []
    for w in range(n_windows):
        rows = slice(64 * w, 64 * w + 64)
        halves = []
        for g in range(2):
            lanes = slice(128 * g, 128 * g + 128)
            kk, vv = k[rows, lanes], v[rows, lanes]
            k_diag = jnp.concatenate([kk * m for m in head_masks], axis=0)
            s = lax.dot_general(
                q[rows, lanes], k_diag, (((1,), (1,)), ((), ())), preferred_element_type=F32
            )
            s = s + bias[:, 256 * g : 256 * g + 256]
            probs = []
            for p in range(2):
                sp = s[:, 128 * p : 128 * p + 128]
                top_lo = jnp.max(jnp.where(low, sp, -jnp.inf), axis=-1, keepdims=True)
                top_hi = jnp.max(jnp.where(low, -jnp.inf, sp), axis=-1, keepdims=True)
                probs.append(jnp.exp2(sp - jnp.where(low, top_lo, top_hi)).astype(BF))
            p4 = jnp.concatenate(probs, axis=1)
            v_diag = jnp.concatenate(
                [jnp.concatenate([vv * m, m], axis=1) for m in head_masks], axis=0
            )
            o = dot(p4, v_diag)
            halves.append(o[:, :128] / o[:, 128:])
        contexts.append(jnp.concatenate(halves, axis=1).astype(BF))
    y = x + dot(jnp.concatenate(contexts, axis=0), w_out[...])
    h = gelu(dot(layer_norm(y, gain_m), w_up[...])).astype(BF)
    return y + dot(h, w_down[...])


def body(
    tokens,
    bn_scale,
    bn_shift,
    w_expand,
    b_expand,
    dw_taps,
    w_project,
    b_project,
    gains,
    w_qkv,
    w_out,
    bias,
    w_up,
    w_down,
    out,
    xf,
    hid,
    taps,
    act,
    conv,
    edge,
    halo_row,
    halo_col,
    halo_hid,
    send,
    recv,
    gathered,
    finished,
    ret,
    halo_send_sem,
    halo_recv_sem,
    go_send_sem,
    go_recv_sem,
    back_send_sem,
    back_recv_sem,
    own_sem,
):
    row = lax.axis_index("row")
    col = lax.axis_index("col")
    core = lax.rem(row, 2)
    pa = row // 2
    me = pa * 8 + col

    def device(index):
        return (2 * (index // 8) + core, lax.rem(index, 8))

    barrier = pltpu.get_barrier_semaphore()

    @pl.loop(1, 64)
    def _(step):
        to_row = 2 * lax.rem(pa + step // 8, 8) + core
        to_col = lax.rem(col + step, 8)
        pl.semaphore_signal(barrier, inc=1, device_id=(to_row, to_col), device_id_type=MESH)

    up, down = lax.rem(row + 15, 16), lax.rem(row + 1, 16)
    left, right = lax.rem(col + 7, 8), lax.rem(col + 1, 8)
    for r in (up, down):
        for c in (left, col, right):
            pl.semaphore_signal(barrier, inc=1, device_id=(r, c), device_id_type=MESH)

    def load_rows(source, at):
        for half in range(2):
            xf[half, pl.ds(pl.multiple_of(at * 256, 256), 256), :] = source[
                :, 128 * half : 128 * half + 128
            ].astype(F32)

    @pl.loop(0, 16)
    def _(r):
        load_rows(tokens[r], r)

    for side in range(2):
        column = [xf[half, pl.ds(255 * side, 16, stride=256), :] for half in range(2)]
        edge[side] = jnp.concatenate(column, axis=1).astype(BF)
    for t in range(10):
        taps[t] = jnp.broadcast_to(dw_taps[t : t + 1, :], (16, 1024)).astype(BF)

    pl.semaphore_wait(barrier, 69)

    halo_copies = []

    def send_halo(src, dst, to):
        n = len(halo_copies)
        copy = pltpu.make_async_remote_copy(
            src_ref=src,
            dst_ref=dst,
            send_sem=halo_send_sem.at[n],
            recv_sem=halo_recv_sem.at[n],
            device_id=to,
            device_id_type=MESH,
        )
        copy.start()
        halo_copies.append(copy)

    send_halo(tokens.at[0], halo_row.at[1], (up, col))
    send_halo(tokens.at[15], halo_row.at[0], (down, col))
    for r, slot in ((up, 2), (row, 1), (down, 0)):
        send_halo(edge.at[0], halo_col.at[1, slot], (r, left))
        send_halo(edge.at[1], halo_col.at[0, slot], (r, right))

    def permuted(at):
        return [
            jnp.concatenate(
                [xf[half, pl.ds(at * 256 + j, 16, stride=16), :] for half in range(2)], axis=1
            )
            for j in range(16)
        ]

    def expand(x, lanes):
        normed = (x * bn_scale[...] + bn_shift[...]).astype(BF)
        return gelu(dot(normed, w_expand[:, lanes]) + b_expand[:, lanes])

    def hidden_row(source, at, mask):
        x = jnp.concatenate(permuted(source), axis=0)
        for n in range(4):
            lanes = slice(256 * n, 256 * n + 256)
            h = expand(x, lanes)
            if mask is not None:
                h = h * mask
            hid[at, 1:17, :, lanes] = h.astype(BF).reshape(16, 16, 256)
            hid[at, 0, :, lanes] = pltpu.roll(h[240:, :], 1, 0).astype(BF)
            hid[at, 17, :, lanes] = pltpu.roll(h[:16, :], 15, 0).astype(BF)

    @pl.loop(0, 16)
    def _(r):
        hidden_row(r, r + 1, None)

    for copy in halo_copies:
        copy.wait()

    top = jnp.where(row > 0, 1.0, 0.0).astype(F32)
    bottom = jnp.where(row < 15, 1.0, 0.0).astype(F32)
    for slot, mask in ((0, top), (1, bottom)):
        load_rows(halo_row[slot], 16 + slot)
        hidden_row(16 + slot, 17 * slot, mask)
    for side, inside in ((0, col > 0), (1, col < 7)):
        x = halo_col[side].reshape(48, 256).astype(F32)
        h = expand(x, slice(0, 1024)) * jnp.where(inside, 1.0, 0.0).astype(F32)
        halo_hid[side] = h
    place = lax.broadcasted_iota(jnp.int32, (16, 1024), 0)

    @pl.loop(0, 18)
    def _(r):
        inside = jnp.where(r == 0, top, jnp.where(r == 17, bottom, 1.0))
        for side in range(2):
            beside = halo_hid[side, pl.ds(15 + r, 1), :] * inside
            old = hid[r, 17 * side].astype(F32)
            hid[r, 17 * side] = jnp.where(place == 15 * side, beside, old).astype(BF)

    lane = lax.broadcasted_iota(jnp.int32, (64, 128), 1) // 32
    head_masks = [jnp.where(lane == h, 1.0, 0.0).astype(BF) for h in range(4)]

    def section(x, i, n_windows):
        return attend_and_mlp(
            x,
            gains[2 * i : 2 * i + 1, :],
            gains[2 * i + 1 : 2 * i + 2, :],
            w_qkv.at[i],
            w_out.at[i],
            bias.at[i],
            w_up.at[i],
            w_down.at[i],
            head_masks,
            n_windows,
        )

    @pl.loop(0, 2)
    def _(band):
        @pl.loop(0, 8)
        def _(r):
            for n in range(8):
                lanes = slice(128 * n, 128 * n + 128)
                weights = [taps[t, :, lanes] for t in range(10)]
                for j in range(16):
                    total = weights[9]
                    for a in range(3):
                        for b in range(3):
                            total = total + hid[band * 8 + r + a, j + b, :, lanes] * weights[3 * a + b]
                    act[16 * j : 16 * j + 16, lanes] = gelu(total.astype(F32)).astype(BF)
            x = jnp.concatenate(permuted(band * 8 + r), axis=0)
            y = x + dot(act[...], w_project[...]) + b_project[...]
            for half in range(2):
                conv[half, pl.ds(pl.multiple_of(r * 256, 256), 256), :] = y[
                    :, 128 * half : 128 * half + 128
                ]

        @pl.loop(0, 8)
        def _(g):
            part = band * 2 + g // 4
            pieces = []
            for s in range(2):
                for jb in range(2):
                    for r in range(8):
                        start = r * 256 + jb * 128 + g * 2 + s
                        pieces.append(
                            jnp.concatenate(
                                [conv[half, pl.ds(start, 8, stride=16), :] for half in range(2)],
                                axis=1,
                            )
                        )
            y = section(jnp.concatenate(pieces, axis=0), 0, 4)
            within = lax.rem(g, 4) * 2
            for s in range(2):
                for r in range(8):
                    at = 128 * s + 8 * r
                    unit = jnp.concatenate([y[at : at + 8], y[at + 64 : at + 72]], axis=0)
                    send[part, r * 8 + within + s] = unit.astype(BF)

            @pl.loop(0, 16)
            def _(u):
                owner = (u // 2) * 8 + within + lax.rem(u, 2)

                @pl.when(owner != me)
                def _():
                    pltpu.make_async_remote_copy(
                        src_ref=send.at[part, owner],
                        dst_ref=recv.at[part, me],
                        send_sem=go_send_sem.at[part],
                        recv_sem=go_recv_sem.at[part],
                        device_id=device(owner),
                        device_id_type=MESH,
                    ).start()

                @pl.when(owner == me)
                def _():
                    recv[part, me] = send[part, owner]

    @pl.loop(0, 4)
    def _(part):
        others = recv.at[part, pl.ds(0, 63)]
        pltpu.make_async_copy(others, others, go_recv_sem.at[part]).wait()

        @pl.loop(0, 4)
        def _(piece):
            block = recv[part, pl.ds(piece * 16, 16)].reshape(256, 256)
            for half in range(2):
                gathered[half, pl.ds(pl.multiple_of(piece * 256, 256), 256), :] = block[
                    :, 128 * half : 128 * half + 128
                ].astype(F32)

        @pl.loop(0, 4)
        def _(g):
            windows = [
                jnp.concatenate(
                    [gathered[half, pl.ds(g * 4 + t, 64, stride=16), :] for half in range(2)], axis=1
                )
                for t in range(4)
            ]
            y = section(jnp.concatenate(windows, axis=0), 1, 4)
            for half in range(2):
                finished[half, pl.ds(pl.multiple_of(g * 256, 256), 256), :] = y[
                    :, 128 * half : 128 * half + 128
                ]

        out_row = (part // 2) * 8 + me // 8
        out_col = pl.multiple_of(lax.rem(part, 2) * 128 + lax.rem(me, 8) * 16, 16)

        @pl.loop(0, 64)
        def _(source):
            unit = [finished[half, pl.ds(source, 16, stride=64), :] for half in range(2)]
            ret[part, source] = jnp.concatenate(unit, axis=1).astype(BF)

            @pl.when(source != me)
            def _():
                pltpu.make_async_remote_copy(
                    src_ref=ret.at[part, source],
                    dst_ref=out.at[out_row, pl.ds(out_col, 16)],
                    send_sem=back_send_sem.at[part],
                    recv_sem=back_recv_sem.at[part],
                    device_id=device(source),
                    device_id_type=MESH,
                ).start()

            @pl.when(source == me)
            def _():
                pltpu.make_async_copy(
                    ret.at[part, source],
                    out.at[out_row, pl.ds(out_col, 16)],
                    own_sem.at[part],
                ).start()

    @pl.loop(0, 4)
    def _(part):
        sent = send.at[part, pl.ds(0, 63)]
        pltpu.make_async_copy(sent, sent, go_send_sem.at[part]).wait()
        back = ret.at[part, pl.ds(0, 63)]
        pltpu.make_async_copy(back, back, back_send_sem.at[part]).wait()
        pltpu.make_async_copy(back, back, back_recv_sem.at[part]).wait()
        pltpu.make_async_copy(ret.at[part, 0], ret.at[part, 0], own_sem.at[part]).wait()


def table_index(window):
    places = jnp.arange(window * window, dtype=jnp.int32)
    across = places // window
    within = places % window
    row_part = (across[:, None] - across[None, :] + window - 1) * (2 * window - 1)
    return row_part + (within[:, None] - within[None, :] + window - 1)


def bias_tables(rel_bias):
    sections, heads, entries = rel_bias.shape
    index = table_index(WIN).reshape(1, -1)
    onehot = (jnp.arange(entries, dtype=jnp.int32)[:, None] == index).astype(F32)
    lookup = jnp.dot(
        rel_bias.reshape(-1, entries) * math.log2(math.e), onehot, precision=lax.Precision.HIGHEST
    )
    lookup = lookup.reshape(sections, heads, 64, 64).transpose(0, 2, 1, 3)
    return lookup.reshape(sections, 64, heads * 64)


def on_device(
    tokens,
    bn_scale,
    bn_shift,
    w_expand,
    b_expand,
    dw_kernel,
    dw_bias,
    w_project,
    b_project,
    norm_gains,
    attn_qkv,
    attn_out,
    rel_bias,
    mlp_up,
    mlp_down,
):
    dw_taps = jnp.concatenate([dw_kernel.reshape(9, 1024), dw_bias.reshape(1, 1024)], axis=0)
    vmem = pl.BlockSpec(memory_space=pltpu.VMEM)
    return pl.pallas_call(
        body,
        out_shape=jax.ShapeDtypeStruct((16, 256, 256), BF),
        in_specs=[vmem] * 14,
        out_specs=pl.BlockSpec(memory_space=pl.ANY),
        scratch_shapes=[
            pltpu.VMEM((2, 18 * 256, 128), F32),
            pltpu.VMEM((18, 18, 16, 1024), BF),
            pltpu.VMEM((10, 16, 1024), BF),
            pltpu.VMEM((256, 1024), BF),
            pltpu.VMEM((2, 8 * 256, 128), F32),
            pltpu.VMEM((2, 16, 256), BF),
            pltpu.VMEM((2, 256, 256), BF),
            pltpu.VMEM((2, 3, 16, 256), BF),
            pltpu.VMEM((2, 48, 1024), F32),
            pltpu.VMEM((4, 64, 16, 256), BF),
            pltpu.VMEM((4, 64, 16, 256), BF),
            pltpu.VMEM((2, 1024, 128), F32),
            pltpu.VMEM((2, 1024, 128), F32),
            pltpu.VMEM((4, 64, 16, 256), BF),
            pltpu.SemaphoreType.DMA((8,)),
            pltpu.SemaphoreType.DMA((8,)),
            pltpu.SemaphoreType.DMA((4,)),
            pltpu.SemaphoreType.DMA((4,)),
            pltpu.SemaphoreType.DMA((4,)),
            pltpu.SemaphoreType.DMA((4,)),
            pltpu.SemaphoreType.DMA((4,)),
        ],
        compiler_params=pltpu.CompilerParams(
            collective_id=0, has_side_effects=True, vmem_limit_bytes=56 * 1024 * 1024
        ),
        cost_estimate=pl.CostEstimate(
            flops=20_000_000_000, bytes_accessed=8_000_000, transcendentals=20_000_000
        ),
        name="maxvit",
    )(
        tokens,
        bn_scale.reshape(1, -1),
        bn_shift.reshape(1, -1),
        w_expand,
        b_expand.reshape(1, -1),
        dw_taps,
        w_project,
        b_project.reshape(1, -1),
        norm_gains,
        attn_qkv,
        attn_out,
        bias_tables(rel_bias),
        mlp_up,
        mlp_down,
    )


def solution(mesh):
    placed = (P("row", "col", None),) + (P(),) * 14
    return jax.shard_map(
        on_device, mesh=mesh, in_specs=placed, out_specs=P("row", "col", None), check_vma=False
    )
```

time: 504 us -> 147 us (0.29)
  Pallas kernels: 0 us -> 135 us
  matrix products: 125 us -> 3.33 us
  other arithmetic: 109 us -> 1.42 us
  blocking collectives: 106 us -> 0 us
  local copies, waits for them, and re-layouts: 110 us -> 4.79 us
  waiting for transfers between devices: 29.9 us -> 0 us
  starting transfers between devices: 16.6 us -> 0 us
    pallas_call x0 -> x1, Pallas kernels: none -> 135 us  [on_device(): pl.pallas_call(body, out_shape=jax.ShapeDtypeStruct((16, 256, 256), BF),...]
    dot_general x14 -> x1, matrix products: 125 us -> 3.33 us  [bias_tables(): jnp.dot(rel_bias.reshape(-1, entries) * math.log2(math.e), onehot, precis...]
    all_to_all x3 -> x0, blocking collectives: 106 us -> none  [the longest x1 41.6 us: on_device(): lax.all_to_all(local_parts.reshape(n_row, n_col, part_windows, -1, featur...]
    reshape x4 -> x2, local copies, waits for them, and re-layouts: 48.6 us -> 1.7 us  [the longest x1 0.88 us: bias_tables(): return lookup.reshape(sections, 64, heads * 64)]
    convert_element_type x10 -> x0, other arithmetic: 43.6 us -> none  [the longest x1 30.6 us: on_device(): jax.nn.gelu(summed).astype(jnp.bfloat16).reshape(tile_r * tile_c, -1)]
    convert_element_type x7 -> x0, local copies, waits for them, and re-layouts: 37.5 us -> none  [the longest x2 17.2 us: attend(): packed = jnp.dot(normed.reshape(-1, features), w_qkv, preferred_element_t...]
    sub x2 -> x0, other arithmetic: 35.6 us -> none  [attend(): weights = jax.nn.softmax(scores, axis=-1).astype(jnp.bfloat16)]
    all_to_all x1 -> x0, waiting for transfers between devices: 24.3 us -> none  [on_device(): lax.all_to_all(lax.all_to_all(local_parts.reshape(n_row, n_col, part_wind...]
  transfers between devices with their start and end apart: 5 -> 0, of which waited for: 3 -> 0; matrix products, arithmetic and copies ran while one was open for 1% -> 0% of each run, Pallas kernels for 0% -> 0%
where the time goes in v1:
time: 147 us; the launch traced here: 145 us
  Pallas kernels  135 us (92%)
  local copies, waits for them, and re-layouts  4.79 us (3%)
  matrix products  3.33 us (2%)
    pallas_call x1, Pallas kernels, on_device(): pl.pallas_call(body, out_shape=jax.ShapeDtypeStruct((16, 256, 256), BF),...  135 us
    dot_general x1, matrix products, bias_tables(): jnp.dot(rel_bias.reshape(-1, entries) * math.log2(math.e), onehot, precis...  3.33 us
    unnamed x1, local copies, waits for them, and re-layouts  3.1 us

profile of v1, /device:TPU:0, one launch (start us, length us, event | category | flops | bytes accessed | tf_op | source)
XLA Modules:
  0.0 144.9 jit_solution(16284051429118346009)
XLA Ops:
  0.0 0.1 add_add_fusion
  0.1 0.8 reshape.108
  0.9 1.3 pad_maximum_fusion.dw_taps
  2.3 3.3 %fusion.4 = f32[2,64,8,64]{3,2,1,0:T(8,128)S(1)} fusion(s32[64,64]{1,0:T(8,128)S(1)} %add_add_fusion, f32[2,8,225]{2,1,0:T(8,128)} %param.27), kind=kOutput, calls=%fused_computation.4 | convolution fusion | flops 177872400 | bytes 292928 | tf_op jit(solution)/shard_map/dot_general | solution.py:372
  5.6 0.9 reshape.111.bias
  6.5 135.3 %maxvit.1 = bf16[16,256,256]{2,1,0:T(8,128)(2,1)} custom-call(bf16[16,256,256]{2,1,0:T(8,128)(2,1)} %tokens.1, f32[1,256]{1,0:T(1,128)} %bitcast.21, f32[1,256]{1,0:T(1,128)} %bitcast.22, bf16[256,1024]{1,0:T(8,128)(2,1)} %w_expand.1, f32[1,1024]{1,0:T(1,128)} %bitcast.20, f32[10,1024]{1,0:T(8,128)} %pad_maximum_fusion.dw_taps, bf16[1024,256]{1,0:T(8,128)(2,1)} %w_project.1, ...), custom_call_target="tpu_custom_call" | custom-call | flops 20000000000 | bytes 8000000 | tf_op jit(solution)/shard_map/maxvit/pallas_call | solution.py:398
  141.8 3.1 %copy.18 = bf16[16,256,256]{2,1,0:T(8,128)(2,1)} copy(bf16[16,256,256]{2,1,0:T(8,128)(2,1)} %maxvit.1) | data formatting | bytes 4194304
  (1 shorter events, 0.0 us)

commit v2 on v1

v2 whole, which is shorter than its diff:
```python
import math

import jax
import jax.numpy as jnp
from jax import lax
from jax.experimental import pallas as pl
from jax.experimental.pallas import tpu as pltpu
from jax.sharding import PartitionSpec as P

WIN = 8
BF = jnp.bfloat16
F32 = jnp.float32
MESH = pl.DeviceIdType.MESH


def gelu_of_half(h):
    h = h.astype(BF)
    inner = h * (BF(2 * 0.7978845608) + BF(8 * 0.0356774081) * (h * h))
    return h + h * jnp.tanh(inner)


def dot(a, b):
    return jnp.dot(a, b, preferred_element_type=F32)


def layer_norm(x, gain):
    center = x - jnp.mean(x, axis=-1, keepdims=True)
    spread = jnp.mean(center * center, axis=-1, keepdims=True)
    return (center * lax.rsqrt(spread + 1e-05) * gain).astype(BF)


def attend(x, gain, w_qkv, w_out, bias, head_masks):
    qkv = dot(layer_norm(x, gain), w_qkv[...])
    q = (qkv[:, :256] * (math.log2(math.e) / math.sqrt(32.0))).astype(BF)
    k = qkv[:, 256:512].astype(BF)
    v = qkv[:, 512:].astype(BF)
    low = lax.broadcasted_iota(jnp.int32, (64, 128), 1) < 64
    contexts = []
    for w in range(x.shape[0] // 64):
        rows = slice(64 * w, 64 * w + 64)
        halves = []
        for g in range(2):
            lanes = slice(128 * g, 128 * g + 128)
            kk, vv = k[rows, lanes], v[rows, lanes]
            k_diag = jnp.concatenate([kk * m for m in head_masks], axis=0)
            s = lax.dot_general(
                q[rows, lanes], k_diag, (((1,), (1,)), ((), ())), preferred_element_type=F32
            )
            s = s + bias[:, 256 * g : 256 * g + 256]
            probs = []
            for p in range(2):
                sp = s[:, 128 * p : 128 * p + 128]
                top_lo = jnp.max(jnp.where(low, sp, -jnp.inf), axis=-1, keepdims=True)
                top_hi = jnp.max(jnp.where(low, -jnp.inf, sp), axis=-1, keepdims=True)
                probs.append(jnp.exp2(sp - jnp.where(low, top_lo, top_hi)).astype(BF))
            p4 = jnp.concatenate(probs, axis=1)
            v_diag = jnp.concatenate(
                [jnp.concatenate([vv * m, m], axis=1) for m in head_masks], axis=0
            )
            o = dot(p4, v_diag)
            halves.append(o[:, :128] / o[:, 128:])
        contexts.append(jnp.concatenate(halves, axis=1).astype(BF))
    return x + dot(jnp.concatenate(contexts, axis=0), w_out[...])


def mlp(y, gain, w_up, w_down):
    h = gelu_of_half(dot(layer_norm(y, gain * 0.5), w_up[...]))
    return y + dot(h, w_down[...])


def fill_bias(rel_bias, split, looked_up, bias):
    rest = rel_bias[...] * math.log2(math.e)
    split[...] = jnp.zeros_like(split)
    for n in range(3):
        piece = rest.astype(BF)
        rest = rest - piece.astype(F32)
        split[16 * n : 16 * n + 16, :225] = piece.astype(F32)
    lane = lax.broadcasted_iota(jnp.int32, (1, 4096), 1)
    q = lax.rem(lane // 64, 2) * 32 + lane // 128
    k = lax.rem(lane, 64)
    entry = (q // 8 - k // 8 + 7) * 15 + lax.rem(q, 8) - lax.rem(k, 8) + 7
    onehot = jnp.where(lax.broadcasted_iota(jnp.int32, (256, 4096), 0) == entry, 1.0, 0.0)
    found = dot(split[...].astype(BF), onehot.astype(BF))
    found = found[:16] + found[16:32] + found[32:]
    for t in range(32):
        looked_up[16 * t : 16 * t + 16, :] = found[:, 128 * t : 128 * t + 128]
    low = lax.broadcasted_iota(jnp.int32, (32, 128), 1) < 64
    for i in range(2):
        for pair in range(4):
            even = looked_up[pl.ds(8 * i + 2 * pair, 32, stride=16), :]
            odd = looked_up[pl.ds(8 * i + 2 * pair + 1, 32, stride=16), :]
            lanes = slice(128 * pair, 128 * pair + 128)
            bias[i, :32, lanes] = jnp.where(low, even, pltpu.roll(odd, 64, 1))
            bias[i, 32:, lanes] = jnp.where(low, pltpu.roll(even, 64, 1), odd)


def body(
    tokens,
    bn_scale,
    bn_shift,
    w_expand,
    b_expand,
    dw_kernel,
    dw_bias,
    w_project,
    b_project,
    gains,
    w_qkv,
    w_out,
    rel_bias,
    w_up,
    w_down,
    out,
    xf,
    hid,
    taps,
    act,
    conv,
    edge,
    halo_row,
    halo_col,
    halo_hid,
    split,
    looked_up,
    bias,
    send,
    recv,
    gathered,
    finished,
    ret,
    back,
    done,
    halo_send_sem,
    halo_recv_sem,
    go_send_sem,
    go_recv_sem,
    back_send_sem,
    back_recv_sem,
    out_sem,
):
    row = lax.axis_index("row")
    col = lax.axis_index("col")
    core = lax.rem(row, 2)
    pa = row // 2
    me = pa * 8 + col

    def device(index):
        return (2 * (index // 8) + core, lax.rem(index, 8))

    barrier = pltpu.get_barrier_semaphore()

    @pl.loop(1, 64)
    def _(step):
        pl.semaphore_signal(
            barrier, inc=1, device_id=device(lax.rem(me + step, 64)), device_id_type=MESH
        )

    up, down = lax.rem(row + 15, 16), lax.rem(row + 1, 16)
    left, right = lax.rem(col + 7, 8), lax.rem(col + 1, 8)
    for r in (up, down):
        for c in (left, col, right):
            pl.semaphore_signal(barrier, inc=1, device_id=(r, c), device_id_type=MESH)

    def load_rows(source, at):
        for half in range(2):
            xf[half, pl.ds(pl.multiple_of(at * 256, 256), 256), :] = source[
                :, 128 * half : 128 * half + 128
            ].astype(F32)

    @pl.loop(0, 16)
    def _(r):
        load_rows(tokens[r], r)

    for side in range(2):
        column = [xf[half, pl.ds(255 * side, 16, stride=256), :] for half in range(2)]
        edge[side] = jnp.concatenate(column, axis=1).astype(BF)
    for t in range(9):
        tap = dw_kernel[t // 3, t % 3 : t % 3 + 1, :]
        taps[t] = jnp.broadcast_to(tap * 0.5, (16, 1024)).astype(BF)
    taps[9] = jnp.broadcast_to(dw_bias[...] * 0.5, (16, 1024)).astype(BF)

    pl.semaphore_wait(barrier, 69)

    halo_copies = []

    def send_halo(src, dst, to):
        n = len(halo_copies)
        copy = pltpu.make_async_remote_copy(
            src_ref=src,
            dst_ref=dst,
            send_sem=halo_send_sem.at[n],
            recv_sem=halo_recv_sem.at[n],
            device_id=to,
            device_id_type=MESH,
        )
        copy.start()
        halo_copies.append(copy)

    send_halo(tokens.at[0], halo_row.at[1], (up, col))
    send_halo(tokens.at[15], halo_row.at[0], (down, col))
    for r, slot in ((up, 2), (row, 1), (down, 0)):
        send_halo(edge.at[0], halo_col.at[1, slot], (r, left))
        send_halo(edge.at[1], halo_col.at[0, slot], (r, right))

    def normed_half(x):
        return (x * (bn_scale[...] * 0.5) + bn_shift[...] * 0.5).astype(BF)

    def expand(normed, lanes):
        return gelu_of_half(dot(normed, w_expand[:, lanes]) + b_expand[:, lanes] * 0.5)

    def hidden_rows(source, at, masks):
        count = len(masks)
        x = [
            jnp.concatenate(
                [xf[half, pl.ds((source + i) * 256 + j, 32, stride=8), :] for half in range(2)],
                axis=1,
            )
            for i in range(count)
            for j in range(8)
        ]
        normed = normed_half(jnp.concatenate(x, axis=0))
        for n in range(4):
            lanes = slice(256 * n, 256 * n + 256)
            rows = expand(normed, lanes)
            for i, mask in enumerate(masks):
                h = rows[256 * i : 256 * i + 256]
                if mask is not None:
                    h = h * mask
                hid[at + i, 1:9, :, lanes] = h.reshape(8, 32, 256)
                first, last = h[:32].astype(F32), h[224:].astype(F32)
                hid[at + i, 0, :, lanes] = pltpu.roll(last, 1, 0).astype(BF)
                hid[at + i, 9, :, lanes] = pltpu.roll(first, 31, 0).astype(BF)

    top = jnp.where(row > 0, 1.0, 0.0).astype(F32)
    bottom = jnp.where(row < 15, 1.0, 0.0).astype(F32)
    place = lax.broadcasted_iota(jnp.int32, (16, 1024), 0)

    def place_edges(r):
        inside = jnp.where(r == 0, top, jnp.where(r == 17, bottom, 1.0))
        for side in range(2):
            beside = halo_hid[side, pl.ds(15 + r, 1), :] * inside
            rows = slice(16 * side, 16 * side + 16)
            old = hid[r, 9 * side, rows].astype(F32)
            hid[r, 9 * side, rows] = jnp.where(place == 15 * side, beside, old).astype(BF)

    fill_bias(rel_bias, split, looked_up, bias)

    @pl.loop(0, 3)
    def _(r):
        hidden_rows(r * 3, r * 3 + 1, [None] * 3)

    for copy in halo_copies:
        copy.wait()

    load_rows(halo_row[1], 16)
    load_rows(halo_row[0], 17)
    hidden_rows(17, 0, [top.astype(BF)])
    for side, inside in ((0, col > 0), (1, col < 7)):
        x = halo_col[side].reshape(48, 256).astype(F32)
        h = expand(normed_half(x), slice(0, 1024)).astype(F32)
        halo_hid[side] = h * jnp.where(inside, 1.0, 0.0).astype(F32)
    pl.loop(0, 10)(place_edges)

    lane = lax.broadcasted_iota(jnp.int32, (64, 128), 1) // 32
    head_masks = [jnp.where(lane == h, 1.0, 0.0).astype(BF) for h in range(4)]

    x_chip, y_chip, z_chip = (col // 4) * 2 + lax.rem(pa, 2), pa // 2, lax.rem(col, 4)

    def push_units(part, source, target, send_sem, recv_sem):
        def push(to_pa, to_x, to_z):
            to_col = (to_x // 2) * 4 + to_z
            pltpu.make_async_remote_copy(
                src_ref=source.at[part, to_pa * 8 + to_col],
                dst_ref=target.at[part, me],
                send_sem=send_sem.at[part],
                recv_sem=recv_sem.at[part],
                device_id=(2 * to_pa + core, to_col),
                device_id_type=MESH,
            ).start()

        to_z = [lax.rem(z_chip + b, 4) for b in range(4)]

        def push_group(a, skip):
            to_y = lax.rem(y_chip + a // 2, 4)
            to_x = lax.rem(x_chip + lax.rem(a, 2), 4)
            opposite = lax.rem(to_x + 2, 4)
            to_pa = to_y * 2 + lax.rem(to_x, 2)
            for b in range(skip, 8):
                push(to_pa, to_x if b < 4 else opposite, to_z[b % 4])

        push_group(0, 1)
        pl.loop(1, 8)(lambda a: push_group(a, 0))

    def conv_part(band, side):
        columns = pl.ds(pl.multiple_of(side * 16, 16), 16)

        @pl.loop(0, 4)
        def _(pair):
            for n in range(8):
                lanes = slice(128 * n, 128 * n + 128)
                weights = [taps[t, :, lanes] for t in range(10)]
                window = [
                    [hid[band * 8 + pair * 2 + a, j, columns, lanes] for a in range(4)]
                    for j in range(10)
                ]
                results = []
                for j in range(8):
                    for i in range(2):
                        total = weights[9]
                        for b in range(3):
                            for a in range(3):
                                total = total + window[j + b][i + a] * weights[3 * a + b]
                        results.append(gelu_of_half(total))
                for j in range(8):
                    for i in range(2):
                        at = pl.multiple_of(pair * 256 + i * 128 + j * 16, 16)
                        act[pl.ds(at, 16), lanes] = results[2 * j + i]

        x = [
            jnp.concatenate(
                [
                    xf[half, pl.ds((band * 8 + r) * 256 + side * 128 + j, 16, stride=8), :]
                    for half in range(2)
                ],
                axis=1,
            )
            for r in range(8)
            for j in range(8)
        ]
        y = jnp.concatenate(x, axis=0) + dot(act[...], w_project[...]) + b_project[...]
        for half in range(2):
            conv[half, :, :] = y[:, 128 * half : 128 * half + 128]

    def block_part(part):
        pieces = [
            jnp.concatenate(
                [conv[half, pl.ds(r * 128 + s, 8, stride=16), :] for half in range(2)], axis=1
            )
            for s in range(16)
            for r in range(8)
        ]
        y = attend(
            jnp.concatenate(pieces, axis=0),
            gains[0:1, :],
            w_qkv.at[0],
            w_out.at[0],
            bias.at[0],
            head_masks,
        )
        y = mlp(y, gains[1:2, :], w_up.at[0], w_down.at[0])
        for s in range(8):
            for r in range(8):
                at = 128 * s + 8 * r
                unit = jnp.concatenate([y[at : at + 8], y[at + 64 : at + 72]], axis=0)
                send[part, r * 8 + s] = unit.astype(BF)

        push_units(part, send, recv, go_send_sem, go_recv_sem)

        recv[part, me] = send[part, me]

    def grid_part(part):
        others = recv.at[part, pl.ds(0, 63)]
        pltpu.make_async_copy(others, others, go_recv_sem.at[part]).wait()

        @pl.loop(0, 4)
        def _(piece):
            block = recv[part, pl.ds(piece * 16, 16)].reshape(256, 256)
            for half in range(2):
                gathered[half, pl.ds(pl.multiple_of(piece * 256, 256), 256), :] = block[
                    :, 128 * half : 128 * half + 128
                ].astype(F32)

        windows = [
            jnp.concatenate([gathered[half, pl.ds(t, 64, stride=16), :] for half in range(2)], axis=1)
            for t in range(16)
        ]
        y = attend(
            jnp.concatenate(windows, axis=0),
            gains[2:3, :],
            w_qkv.at[1],
            w_out.at[1],
            bias.at[1],
            head_masks,
        )
        for half in range(2):
            finished[half, :, :] = y[:, 128 * half : 128 * half + 128]
        for source in range(64):
            unit = [finished[half, pl.ds(source, 16, stride=64), :] for half in range(2)]
            ret[part, source] = jnp.concatenate(unit, axis=1).astype(BF)

        push_units(part, ret, back, back_send_sem, back_recv_sem)

        back[part, me] = ret[part, me]

    @pl.loop(0, 5)
    def _(step):
        @pl.when(step == 2)
        def _():
            @pl.loop(0, 2)
            def _(r):
                hidden_rows(r * 3 + 9, r * 3 + 10, [None] * 3)

            hidden_rows(15, 16, [None, bottom.astype(BF)])
            pl.loop(10, 18)(place_edges)

        @pl.when(step < 4)
        def _():
            conv_part(step // 2, lax.rem(step, 2))
            block_part(step)

        @pl.when(step >= 1)
        def _():
            grid_part(step - 1)

    def store(part):
        return pltpu.make_async_copy(
            done.at[part],
            out.at[
                pl.ds((part // 2) * 8, 8), pl.ds(pl.multiple_of(lax.rem(part, 2) * 128, 128), 128)
            ],
            out_sem.at[part],
        )

    @pl.loop(0, 4)
    def _(part):
        others = back.at[part, pl.ds(0, 63)]
        pltpu.make_async_copy(others, others, back_recv_sem.at[part]).wait()
        y = back[part].reshape(1024, 256).astype(F32)
        y = mlp(y, gains[3:4, :], w_up.at[1], w_down.at[1])
        done[part] = y.astype(BF).reshape(8, 128, 256)
        store(part).start()

    @pl.loop(0, 4)
    def _(part):
        sent = send.at[part, pl.ds(0, 63)]
        pltpu.make_async_copy(sent, sent, go_send_sem.at[part]).wait()
        returned = ret.at[part, pl.ds(0, 63)]
        pltpu.make_async_copy(returned, returned, back_send_sem.at[part]).wait()
        store(part).wait()


def on_device(
    tokens,
    bn_scale,
    bn_shift,
    w_expand,
    b_expand,
    dw_kernel,
    dw_bias,
    w_project,
    b_project,
    norm_gains,
    attn_qkv,
    attn_out,
    rel_bias,
    mlp_up,
    mlp_down,
):
    vmem = pl.BlockSpec(memory_space=pltpu.VMEM)
    units = pltpu.VMEM((4, 64, 16, 256), BF)
    return pl.pallas_call(
        body,
        out_shape=jax.ShapeDtypeStruct((16, 256, 256), BF),
        in_specs=[vmem] * 15,
        out_specs=pl.BlockSpec(memory_space=pl.ANY),
        scratch_shapes=[
            pltpu.VMEM((2, 18 * 256, 128), F32),
            pltpu.VMEM((18, 10, 32, 1024), BF),
            pltpu.VMEM((10, 16, 1024), BF),
            pltpu.VMEM((1024, 1024), BF),
            pltpu.VMEM((2, 1024, 128), F32),
            pltpu.VMEM((2, 16, 256), BF),
            pltpu.VMEM((2, 256, 256), BF),
            pltpu.VMEM((2, 3, 16, 256), BF),
            pltpu.VMEM((2, 48, 1024), F32),
            pltpu.VMEM((48, 256), F32),
            pltpu.VMEM((512, 128), F32),
            pltpu.VMEM((2, 64, 512), F32),
            units,
            units,
            pltpu.VMEM((2, 1024, 128), F32),
            pltpu.VMEM((2, 1024, 128), F32),
            units,
            units,
            pltpu.VMEM((4, 8, 128, 256), BF),
            pltpu.SemaphoreType.DMA((8,)),
            pltpu.SemaphoreType.DMA((8,)),
            pltpu.SemaphoreType.DMA((4,)),
            pltpu.SemaphoreType.DMA((4,)),
            pltpu.SemaphoreType.DMA((4,)),
            pltpu.SemaphoreType.DMA((4,)),
            pltpu.SemaphoreType.DMA((4,)),
        ],
        compiler_params=pltpu.CompilerParams(
            collective_id=0, has_side_effects=True, vmem_limit_bytes=60 * 1024 * 1024
        ),
        cost_estimate=pl.CostEstimate(
            flops=20_000_000_000, bytes_accessed=8_000_000, transcendentals=20_000_000
        ),
        name="maxvit",
    )(
        tokens,
        bn_scale.reshape(1, -1),
        bn_shift.reshape(1, -1),
        w_expand,
        b_expand.reshape(1, -1),
        dw_kernel,
        dw_bias.reshape(1, -1),
        w_project,
        b_project.reshape(1, -1),
        norm_gains,
        attn_qkv,
        attn_out,
        rel_bias.reshape(16, 225),
        mlp_up,
        mlp_down,
    )


def solution(mesh):
    placed = (P("row", "col", None),) + (P(),) * 14
    return jax.shard_map(
        on_device, mesh=mesh, in_specs=placed, out_specs=P("row", "col", None), check_vma=False
    )
```

time: 147 us -> 102 us (0.69); the launches traced: 145 us -> 102 us
  Pallas kernels: 135 us -> 99.2 us
  matrix products: 3.33 us -> 0 us
  local copies, waits for them, and re-layouts: 4.79 us -> 3.1 us
    pallas_call x1, Pallas kernels: 135 us -> 99.2 us  [on_device(): pl.pallas_call(body, out_shape=jax.ShapeDtypeStruct((16, 256, 256), BF),...]
    dot_general x1 -> x0, matrix products: 3.33 us -> none  [bias_tables(): jnp.dot(rel_bias.reshape(-1, entries) * math.log2(math.e), onehot, precis...]
    reshape x2 -> x0, local copies, waits for them, and re-layouts: 1.7 us -> none  [the longest x1 0.88 us: bias_tables(): return lookup.reshape(sections, 64, heads * 64)]
where the time goes in v2:
time: 102 us
  Pallas kernels  99.2 us (97%)
  local copies, waits for them, and re-layouts  3.1 us (3%)
    pallas_call x1, Pallas kernels, on_device(): pl.pallas_call(body, out_shape=jax.ShapeDtypeStruct((16, 256, 256), BF),...  99.2 us
    unnamed x1, local copies, waits for them, and re-layouts  3.1 us

profile of v2, /device:TPU:0, one launch (start us, length us, event | category | flops | bytes accessed | tf_op | source)
XLA Modules:
  0.0 102.3 jit_solution(9295740361577832408)
XLA Ops:
  0.0 99.2 %maxvit.1 = bf16[16,256,256]{2,1,0:T(8,128)(2,1)} custom-call(bf16[16,256,256]{2,1,0:T(8,128)(2,1)} %tokens.1, f32[1,256]{1,0:T(1,128)} %bitcast.9, f32[1,256]{1,0:T(1,128)} %bitcast.10, bf16[256,1024]{1,0:T(8,128)(2,1)} %w_expand.1, f32[1,1024]{1,0:T(1,128)} %bitcast.7, f32[3,3,1024]{2,1,0:T(4,128)} %dw_kernel.1, f32[1,1024]{1,0:T(1,128)} %bitcast.8, ...), custom_call_target="tpu_custom_call" | custom-call | flops 20000000000 | bytes 8000000 | tf_op jit(solution)/shard_map/maxvit/pallas_call | solution.py:461
  99.2 3.1 %copy.17 = bf16[16,256,256]{2,1,0:T(8,128)(2,1)} copy(bf16[16,256,256]{2,1,0:T(8,128)(2,1)} %maxvit.1) | data formatting | bytes 4194304

commit v3 on v2

--- a/solution.py
+++ b/solution.py
@@ -35,31 +35,39 @@
     k = qkv[:, 256:512].astype(BF)
     v = qkv[:, 512:].astype(BF)
     low = lax.broadcasted_iota(jnp.int32, (64, 128), 1) < 64
-    contexts = []
-    for w in range(x.shape[0] // 64):
-        rows = slice(64 * w, 64 * w + 64)
-        halves = []
-        for g in range(2):
-            lanes = slice(128 * g, 128 * g + 128)
-            kk, vv = k[rows, lanes], v[rows, lanes]
-            k_diag = jnp.concatenate([kk * m for m in head_masks], axis=0)
-            s = lax.dot_general(
-                q[rows, lanes], k_diag, (((1,), (1,)), ((), ())), preferred_element_type=F32
-            )
-            s = s + bias[:, 256 * g : 256 * g + 256]
-            probs = []
-            for p in range(2):
-                sp = s[:, 128 * p : 128 * p + 128]
-                top_lo = jnp.max(jnp.where(low, sp, -jnp.inf), axis=-1, keepdims=True)
-                top_hi = jnp.max(jnp.where(low, -jnp.inf, sp), axis=-1, keepdims=True)
-                probs.append(jnp.exp2(sp - jnp.where(low, top_lo, top_hi)).astype(BF))
-            p4 = jnp.concatenate(probs, axis=1)
-            v_diag = jnp.concatenate(
-                [jnp.concatenate([vv * m, m], axis=1) for m in head_masks], axis=0
-            )
-            o = dot(p4, v_diag)
-            halves.append(o[:, :128] / o[:, 128:])
-        contexts.append(jnp.concatenate(halves, axis=1).astype(BF))
+    n_windows = x.shape[0] // 64
+    pairs = [(w, g) for w in range(n_windows) for g in range(2)]
+
+    def scores(w, g):
+        rows, lanes = slice(64 * w, 64 * w + 64), slice(128 * g, 128 * g + 128)
+        kk = k[rows, lanes]
+        k_diag = jnp.concatenate([kk * m for m in head_masks], axis=0)
+        return lax.dot_general(
+            q[rows, lanes], k_diag, (((1,), (1,)), ((), ())), preferred_element_type=F32
+        )
+
+    def probabilities(s, g):
+        s = s + bias[:, 256 * g : 256 * g + 256]
+        probs = []
+        for p in range(2):
+            sp = s[:, 128 * p : 128 * p + 128]
+            top_lo = jnp.max(jnp.where(low, sp, -jnp.inf), axis=-1, keepdims=True)
+            top_hi = jnp.max(jnp.where(low, -jnp.inf, sp), axis=-1, keepdims=True)
+            probs.append(jnp.exp2(sp - jnp.where(low, top_lo, top_hi)).astype(BF))
+        return jnp.concatenate(probs, axis=1)
+
+    def context(p4, w, g):
+        vv = v[64 * w : 64 * w + 64, 128 * g : 128 * g + 128]
+        v_diag = jnp.concatenate([jnp.concatenate([vv * m, m], axis=1) for m in head_masks], axis=0)
+        o = dot(p4, v_diag)
+        return (o[:, :128] / o[:, 128:]).astype(BF)
+
+    found = [scores(w, g) for w, g in pairs]
+    found = [probabilities(s, g) for s, (w, g) in zip(found, pairs)]
+    halves = [context(p4, w, g) for p4, (w, g) in zip(found, pairs)]
+    contexts = [
+        jnp.concatenate(halves[2 * w : 2 * w + 2], axis=1) for w in range(n_windows)
+    ]
     return x + dot(jnp.concatenate(contexts, axis=0), w_out[...])
 
 
@@ -95,22 +103,29 @@
 
 
 def body(
-    tokens,
+    tokens_hbm,
     bn_scale,
     bn_shift,
-    w_expand,
+    w_expand_hbm,
     b_expand,
     dw_kernel,
     dw_bias,
-    w_project,
+    w_project_hbm,
     b_project,
     gains,
+    w_qkv_hbm,
+    w_out_hbm,
+    rel_bias,
+    w_up_hbm,
+    w_down_hbm,
+    out,
+    tokens,
+    w_expand,
+    w_project,
     w_qkv,
     w_out,
-    rel_bias,
     w_up,
     w_down,
-    out,
     xf,
     hid,
     taps,
@@ -137,6 +152,7 @@
     back_send_sem,
     back_recv_sem,
     out_sem,
+    load_sem,
 ):
     row = lax.axis_index("row")
     col = lax.axis_index("col")
@@ -147,6 +163,23 @@
     def device(index):
         return (2 * (index // 8) + core, lax.rem(index, 8))
 
+    loads = [
+        pltpu.make_async_copy(source, target, load_sem.at[n])
+        for n, (source, target) in enumerate(
+            (
+                (tokens_hbm, tokens),
+                (w_expand_hbm, w_expand),
+                (w_project_hbm, w_project),
+                (w_qkv_hbm, w_qkv),
+                (w_out_hbm, w_out),
+                (w_up_hbm, w_up),
+                (w_down_hbm, w_down),
+            )
+        )
+    ]
+    for load in loads:
+        load.start()
+
     barrier = pltpu.get_barrier_semaphore()
 
     @pl.loop(1, 64)
@@ -166,6 +199,8 @@
             xf[half, pl.ds(pl.multiple_of(at * 256, 256), 256), :] = source[
                 :, 128 * half : 128 * half + 128
             ].astype(F32)
+
+    loads[0].wait()
 
     @pl.loop(0, 16)
     def _(r):
@@ -244,8 +279,9 @@
             hid[r, 9 * side, rows] = jnp.where(place == 15 * side, beside, old).astype(BF)
 
     fill_bias(rel_bias, split, looked_up, bias)
-
-    @pl.loop(0, 3)
+    loads[1].wait()
+
+    @pl.loop(0, 5)
     def _(r):
         hidden_rows(r * 3, r * 3 + 1, [None] * 3)
 
@@ -392,14 +428,13 @@
 
         back[part, me] = ret[part, me]
 
+    for load in loads[2:]:
+        load.wait()
+
     @pl.loop(0, 5)
     def _(step):
         @pl.when(step == 2)
         def _():
-            @pl.loop(0, 2)
-            def _(r):
-                hidden_rows(r * 3 + 9, r * 3 + 10, [None] * 3)
-
             hidden_rows(15, 16, [None, bottom.astype(BF)])
             pl.loop(10, 18)(place_edges)
 
@@ -457,13 +492,21 @@
     mlp_down,
 ):
     vmem = pl.BlockSpec(memory_space=pltpu.VMEM)
+    hbm = pl.BlockSpec(memory_space=pl.ANY)
     units = pltpu.VMEM((4, 64, 16, 256), BF)
     return pl.pallas_call(
         body,
         out_shape=jax.ShapeDtypeStruct((16, 256, 256), BF),
-        in_specs=[vmem] * 15,
+        in_specs=[hbm, vmem, vmem, hbm, vmem, vmem, vmem, hbm, vmem, vmem, hbm, hbm, vmem, hbm, hbm],
         out_specs=pl.BlockSpec(memory_space=pl.ANY),
         scratch_shapes=[
+            pltpu.VMEM((16, 256, 256), BF),
+            pltpu.VMEM((256, 1024), BF),
+            pltpu.VMEM((1024, 256), BF),
+            pltpu.VMEM((2, 256, 768), BF),
+            pltpu.VMEM((2, 256, 256), BF),
+            pltpu.VMEM((2, 256, 1024), BF),
+            pltpu.VMEM((2, 1024, 256), BF),
             pltpu.VMEM((2, 18 * 256, 128), F32),
             pltpu.VMEM((18, 10, 32, 1024), BF),
             pltpu.VMEM((10, 16, 1024), BF),
@@ -490,6 +533,7 @@
             pltpu.SemaphoreType.DMA((4,)),
             pltpu.SemaphoreType.DMA((4,)),
             pltpu.SemaphoreType.DMA((4,)),
+            pltpu.SemaphoreType.DMA((7,)),
         ],
         compiler_params=pltpu.CompilerParams(
             collective_id=0, has_side_effects=True, vmem_limit_bytes=60 * 1024 * 1024

time: 102 us -> 95.2 us (0.933)
  Pallas kernels: 99.2 us -> 92 us
    pallas_call x1, Pallas kernels: 99.2 us -> 92 us  [on_device(): pl.pallas_call(body, out_shape=jax.ShapeDtypeStruct((16, 256, 256), BF),...]
where the time goes in v3:
time: 95.2 us; the launch traced here: 95.1 us
  Pallas kernels  92 us (97%)
  local copies, waits for them, and re-layouts  3.1 us (3%)
    pallas_call x1, Pallas kernels, on_device(): pl.pallas_call(body, out_shape=jax.ShapeDtypeStruct((16, 256, 256), BF),...  92 us
    unnamed x1, local copies, waits for them, and re-layouts  3.1 us

profile of v3, /device:TPU:0, one launch (start us, length us, event | category | flops | bytes accessed | tf_op | source)
XLA Modules:
  0.0 95.1 jit_solution(7547452372317726539)
XLA Ops:
  0.0 92.0 %maxvit.1 = bf16[16,256,256]{2,1,0:T(8,128)(2,1)} custom-call(bf16[16,256,256]{2,1,0:T(8,128)(2,1)} %tokens_hbm.1, f32[1,256]{1,0:T(1,128)} %bitcast.9, f32[1,256]{1,0:T(1,128)} %bitcast.10, bf16[256,1024]{1,0:T(8,128)(2,1)} %w_expand_hbm.1, f32[1,1024]{1,0:T(1,128)} %bitcast.7, f32[3,3,1024]{2,1,0:T(4,128)} %dw_kernel.1, f32[1,1024]{1,0:T(1,128)} %bitcast.8, ...), custom_call_target="tpu_custom_call" | custom-call | flops 20000000000 | bytes 8000000 | tf_op jit(solution)/shard_map/maxvit/pallas_call | solution.py:497
  92.0 3.1 %copy.17 = bf16[16,256,256]{2,1,0:T(8,128)(2,1)} copy(bf16[16,256,256]{2,1,0:T(8,128)(2,1)} %maxvit.1) | data formatting | bytes 4194304

commit v4 on v3

--- a/solution.py
+++ b/solution.py
@@ -271,9 +271,10 @@
     place = lax.broadcasted_iota(jnp.int32, (16, 1024), 0)
 
     def place_edges(r):
-        inside = jnp.where(r == 0, top, jnp.where(r == 17, bottom, 1.0))
         for side in range(2):
-            beside = halo_hid[side, pl.ds(15 + r, 1), :] * inside
+            beside = halo_hid[side, 15 + r : 16 + r, :]
+            if r in (0, 17):
+                beside = beside * (top if r == 0 else bottom)
             rows = slice(16 * side, 16 * side + 16)
             old = hid[r, 9 * side, rows].astype(F32)
             hid[r, 9 * side, rows] = jnp.where(place == 15 * side, beside, old).astype(BF)
@@ -295,16 +296,26 @@
         x = halo_col[side].reshape(48, 256).astype(F32)
         h = expand(normed_half(x), slice(0, 1024)).astype(F32)
         halo_hid[side] = h * jnp.where(inside, 1.0, 0.0).astype(F32)
-    pl.loop(0, 10)(place_edges)
+    for r in range(10):
+        place_edges(r)
 
     lane = lax.broadcasted_iota(jnp.int32, (64, 128), 1) // 32
     head_masks = [jnp.where(lane == h, 1.0, 0.0).astype(BF) for h in range(4)]
 
     x_chip, y_chip, z_chip = (col // 4) * 2 + lax.rem(pa, 2), pa // 2, lax.rem(col, 4)
 
+    to_x = [lax.rem(x_chip + d, 4) for d in range(4)]
+    to_y = [lax.rem(y_chip + d, 4) for d in range(4)]
+    to_z = [lax.rem(z_chip + d, 4) for d in range(4)]
+    offsets = sorted(
+        ((y, x, z) for y in range(4) for x in range(4) for z in range(4)),
+        key=lambda o: (-sum(min(d, 4 - d) for d in o), (o[0] + o[1] + 2 * o[2]) % 4, o),
+    )[:-1]
+
     def push_units(part, source, target, send_sem, recv_sem):
-        def push(to_pa, to_x, to_z):
-            to_col = (to_x // 2) * 4 + to_z
+        for y, x, z in offsets:
+            to_pa = to_y[y] * 2 + lax.rem(to_x[x], 2)
+            to_col = (to_x[x] // 2) * 4 + to_z[z]
             pltpu.make_async_remote_copy(
                 src_ref=source.at[part, to_pa * 8 + to_col],
                 dst_ref=target.at[part, me],
@@ -313,19 +324,6 @@
                 device_id=(2 * to_pa + core, to_col),
                 device_id_type=MESH,
             ).start()
-
-        to_z = [lax.rem(z_chip + b, 4) for b in range(4)]
-
-        def push_group(a, skip):
-            to_y = lax.rem(y_chip + a // 2, 4)
-            to_x = lax.rem(x_chip + lax.rem(a, 2), 4)
-            opposite = lax.rem(to_x + 2, 4)
-            to_pa = to_y * 2 + lax.rem(to_x, 2)
-            for b in range(skip, 8):
-                push(to_pa, to_x if b < 4 else opposite, to_z[b % 4])
-
-        push_group(0, 1)
-        pl.loop(1, 8)(lambda a: push_group(a, 0))
 
     def conv_part(band, side):
         columns = pl.ds(pl.multiple_of(side * 16, 16), 16)
@@ -431,21 +429,22 @@
     for load in loads[2:]:
         load.wait()
 
-    @pl.loop(0, 5)
+    @pl.loop(0, 6)
     def _(step):
         @pl.when(step == 2)
         def _():
             hidden_rows(15, 16, [None, bottom.astype(BF)])
-            pl.loop(10, 18)(place_edges)
+            for r in range(10, 18):
+                place_edges(r)
 
         @pl.when(step < 4)
         def _():
             conv_part(step // 2, lax.rem(step, 2))
             block_part(step)
 
-        @pl.when(step >= 1)
+        @pl.when(step >= 2)
         def _():
-            grid_part(step - 1)
+            grid_part(step - 2)
 
     def store(part):
         return pltpu.make_async_copy(

time: 95.2 us -> 93.1 us (0.978)
  Pallas kernels: 92 us -> 89.3 us
    pallas_call x1, Pallas kernels: 92 us -> 89.3 us  [on_device(): pl.pallas_call(body, out_shape=jax.ShapeDtypeStruct((16, 256, 256), BF),...]
where the time goes in v4:
time: 93.1 us; the launch traced here: 92.4 us
  Pallas kernels  89.3 us (96%)
  local copies, waits for them, and re-layouts  3.1 us (3%)
    pallas_call x1, Pallas kernels, on_device(): pl.pallas_call(body, out_shape=jax.ShapeDtypeStruct((16, 256, 256), BF),...  89.3 us
    unnamed x1, local copies, waits for them, and re-layouts  3.1 us

profile of v4, /device:TPU:0, one launch (start us, length us, event | category | flops | bytes accessed | tf_op | source)
XLA Modules:
  0.0 92.4 jit_solution(17517768159764818984)
XLA Ops:
  0.0 89.3 %maxvit.1 = bf16[16,256,256]{2,1,0:T(8,128)(2,1)} custom-call(bf16[16,256,256]{2,1,0:T(8,128)(2,1)} %tokens_hbm.1, f32[1,256]{1,0:T(1,128)} %bitcast.9, f32[1,256]{1,0:T(1,128)} %bitcast.10, bf16[256,1024]{1,0:T(8,128)(2,1)} %w_expand_hbm.1, f32[1,1024]{1,0:T(1,128)} %bitcast.7, f32[3,3,1024]{2,1,0:T(4,128)} %dw_kernel.1, f32[1,1024]{1,0:T(1,128)} %bitcast.8, ...), custom_call_target="tpu_custom_call" | custom-call | flops 20000000000 | bytes 8000000 | tf_op jit(solution)/shard_map/maxvit/pallas_call | solution.py:496
  89.3 3.1 %copy.17 = bf16[16,256,256]{2,1,0:T(8,128)(2,1)} copy(bf16[16,256,256]{2,1,0:T(8,128)(2,1)} %maxvit.1) | data formatting | bytes 4194304

commit v5 on v4

--- a/solution.py
+++ b/solution.py
@@ -202,7 +202,7 @@
 
     loads[0].wait()
 
-    @pl.loop(0, 16)
+    @pl.loop(0, 16, unroll=4)
     def _(r):
         load_rows(tokens[r], r)
 
@@ -213,6 +213,8 @@
         tap = dw_kernel[t // 3, t % 3 : t % 3 + 1, :]
         taps[t] = jnp.broadcast_to(tap * 0.5, (16, 1024)).astype(BF)
     taps[9] = jnp.broadcast_to(dw_bias[...] * 0.5, (16, 1024)).astype(BF)
+
+    fill_bias(rel_bias, split, looked_up, bias)
 
     pl.semaphore_wait(barrier, 69)
 
@@ -279,7 +281,6 @@
             old = hid[r, 9 * side, rows].astype(F32)
             hid[r, 9 * side, rows] = jnp.where(place == 15 * side, beside, old).astype(BF)
 
-    fill_bias(rel_bias, split, looked_up, bias)
     loads[1].wait()
 
     @pl.loop(0, 5)

time: 93.1 us -> 94.1 us (1.011); the launches traced: 92.4 us -> 92.4 us
  no operation moved by 1% of the time
where the time goes in v5:
time: 94.1 us; the launch traced here: 92.4 us
  Pallas kernels  89.3 us (95%)
  local copies, waits for them, and re-layouts  3.1 us (3%)
    pallas_call x1, Pallas kernels, on_device(): pl.pallas_call(body, out_shape=jax.ShapeDtypeStruct((16, 256, 256), BF),...  89.3 us
    unnamed x1, local copies, waits for them, and re-layouts  3.1 us

profile of v5, /device:TPU:0, one launch (start us, length us, event | category | flops | bytes accessed | tf_op | source)
XLA Modules:
  0.0 92.4 jit_solution(8089427905553966325)
XLA Ops:
  0.0 89.3 %maxvit.1 = bf16[16,256,256]{2,1,0:T(8,128)(2,1)} custom-call(bf16[16,256,256]{2,1,0:T(8,128)(2,1)} %tokens_hbm.1, f32[1,256]{1,0:T(1,128)} %bitcast.9, f32[1,256]{1,0:T(1,128)} %bitcast.10, bf16[256,1024]{1,0:T(8,128)(2,1)} %w_expand_hbm.1, f32[1,1024]{1,0:T(1,128)} %bitcast.7, f32[3,3,1024]{2,1,0:T(4,128)} %dw_kernel.1, f32[1,1024]{1,0:T(1,128)} %bitcast.8, ...), custom_call_target="tpu_custom_call" | custom-call | flops 20000000000 | bytes 8000000 | tf_op jit(solution)/shard_map/maxvit/pallas_call | solution.py:497
  89.3 3.1 %copy.17 = bf16[16,256,256]{2,1,0:T(8,128)(2,1)} copy(bf16[16,256,256]{2,1,0:T(8,128)(2,1)} %maxvit.1) | data formatting | bytes 4194304
